TPU v7x, 256 devices: a whole 4x4x8 slice. The times are simulated.
256 devices in a mesh: dp: 8 (over x, core), tensor: 32 (over y, z).
Axes of the slice: x: 4, y: 4, z: 8, core: 2. Of those that a mesh axis runs over, the one named last changes fastest.
Arguments:
- out_grad: bfloat16 [1024, 16384], P('tensor', 'dp'), may hold values from -6 to 6
- down_weight: bfloat16 [53248, 16384], P('tensor', 'dp'), may hold values from -0.046875 to 0.046875
- gate_pre: bfloat16 [1024, 53248], P('dp', 'tensor'), may hold values from -6 to 6
- inputs: bfloat16 [1024, 16384], P('dp', 'tensor'), may hold values from -6 to 6
- test_matrix: bfloat16 [53248, 128], P('tensor'), may hold values from -0.02734375 to 0.02734375
Outputs:
- basis: float32 [16384, 128], P('tensor')
- corange: float32 [128, 53248], P(None, 'tensor')
All inputs are finite; a program needn't handle non-finite values.
Results may differ from a plain program's by a relative error of at most 0.0044.
Values may be sent and summed in bfloat16 or wider, within the bound.
A program may use at most 64 MiB of HBM per device.

v0:
```python
import math

import jax
import jax.numpy as jnp
from jax import lax
from jax.sharding import PartitionSpec as P

D = 16384


def orthonormal(range_cols, gram):
    lower = jnp.linalg.cholesky(gram)
    return lax.linalg.triangular_solve(
        lower, range_cols, left_side=False, lower=True, transpose_a=True
    )


def shards(out_grad, down_weight, gate_pre, inputs, test_matrix):
    gathered = lax.all_gather(out_grad, "tensor", axis=0, tiled=True)
    tokens_all = gathered.shape[0]
    own_rows = gate_pre.shape[0]
    factor = 1.0 / math.sqrt(tokens_all)
    partial_all = lax.dot_general(
        gathered, down_weight, (((1,), (1,)), ((), ())), preferred_element_type=jnp.float32
    )
    summed = lax.psum(partial_all, "dp")
    hidden_grad = lax.dynamic_slice_in_dim(summed, lax.axis_index("dp") * own_rows, own_rows, 0)
    up_grad = (hidden_grad * jax.nn.silu(gate_pre.astype(jnp.float32))).astype(jnp.bfloat16)
    sketch_part = jnp.dot(up_grad, test_matrix, preferred_element_type=jnp.float32)
    sketch = lax.psum(sketch_part, "tensor")
    inputs_wide = inputs.astype(jnp.float32)
    range_part = lax.dot_general(
        inputs_wide, sketch, (((0,), (0,)), ((), ())), precision=lax.Precision.HIGHEST
    )
    range_cols = lax.psum(range_part, "dp") * factor
    gram_local = jnp.dot(range_cols.T, range_cols, precision=lax.Precision.HIGHEST)
    gram = lax.psum(gram_local, "tensor")
    ortho = orthonormal(range_cols, gram)
    basis = ortho * math.sqrt(D)
    coeff_part = jnp.dot(inputs_wide, ortho, precision=lax.Precision.HIGHEST)
    coeff = lax.psum(coeff_part, "tensor")
    corange_part = lax.dot_general(
        coeff,
        up_grad.astype(jnp.float32),
        (((0,), (0,)), ((), ())),
        precision=lax.Precision.HIGHEST,
    )
    corange = lax.psum(corange_part, "dp") * factor
    return (basis, corange)


def solution(mesh):
    return jax.shard_map(
        shards,
        mesh=mesh,
        in_specs=(
            P("tensor", "dp"),
            P("tensor", "dp"),
            P("dp", "tensor"),
            P("dp", "tensor"),
            P("tensor", None),
        ),
        out_specs=(P("tensor", None), P(None, "tensor")),
        check_vma=False,
    )
```

profile of v0, /device:TPU:1, one launch (start us, length us, event | category | flops | bytes accessed | tf_op | source)
XLA Modules:
  0.0 793.0 jit_solution(17904724952345475580)
XLA Ops:
  7.2 0.0 all-gather.2.cloned.1.call-start
  7.2 0.7 all-gather.2.cloned.1.call-update
  7.9 0.0 all-reduce.7.cloned.1.call-start
  8.0 85.6 %all-gather.2.cloned.1.call-done = bf16[1024,2048]{1,0:T(8,128)(2,1)} async-done(((bf16[32,2048]{1,0:T(8,128)(2,1)}), bf16[1024,2048]{1,0:T(8,128)(2,1)}) %all-gather.2.cloned.1.call-update) | async-done | bytes 4194320 | tf_op jit(solution)/shard_map/all_gather | solution.py:19
  93.6 13.3 %fusion.16 = f32[1024,1664]{1,0:T(8,128)} fusion(bf16[1024,2048]{1,0:T(8,128)(2,1)} %all-gather.2.cloned.1.call-done, bf16[1664,2048]{1,0:T(8,128)(2,1)} %param.6), kind=kOutput, calls=%fused_computation.28 | convolution fusion | flops 6979321856 | bytes 17825792 | tf_op jit(solution)/shard_map/dot_general | solution.py:23
  106.9 0.0 all-reduce.7.cloned.1.call-update
  107.0 0.0 all-reduce.9.cloned.1.call-start
  107.0 93.8 %all-reduce.7.cloned.1.call-done = f32[1024,1664]{1,0:T(8,128)} async-done(((f32[1024,1664]{1,0:T(8,128)}), f32[1024,1664]{1,0:T(8,128)}) %all-reduce.7.cloned.1.call-update) | async-done | bytes 6815760 | tf_op jit(solution)/shard_map/psum | solution.py:26
  200.8 1.4 fusion.4
  202.2 0.9 fusion.17
  203.1 0.0 all-reduce.11.cloned.1.call-start
  203.2 136.9 %all-reduce.9.cloned.1.call-done = f32[128,128]{1,0:T(8,128)} async-done(((f32[128,128]{1,0:T(8,128)}), f32[128,128]{1,0:T(8,128)}) %all-reduce.9.cloned.1.call-update) | async-done | bytes 65552 | tf_op jit(solution)/shard_map/psum | solution.py:30
  340.0 1.9 convolution_bitcast_fusion
  341.9 0.0 all-reduce.11.cloned.1.call-update
  341.9 0.0 all-reduce.13.cloned.1.call-start
  342.0 66.0 %all-reduce.11.cloned.1.call-done = f32[512,128]{0,1:T(8,128)} async-done(((f32[512,128]{0,1:T(8,128)}), f32[512,128]{0,1:T(8,128)}) %all-reduce.11.cloned.1.call-update) | async-done | bytes 262160 | tf_op jit(solution)/shard_map/psum | solution.py:35
  407.9 2.0 fusion.7
  410.0 0.0 all-reduce.15.cloned.1.call-start
  410.0 138.4 %all-reduce.13.cloned.1.call-done = f32[128,128]{0,1:T(8,128)} async-done(((f32[128,128]{0,1:T(8,128)}), f32[128,128]{0,1:T(8,128)}) %all-reduce.13.cloned.1.call-update) | async-done | bytes 65552 | tf_op jit(solution)/shard_map/psum | solution.py:37
  548.4 0.9 copy.8
  549.4 0.9 fusion.13
  550.2 11.7 %cholesky.16 = f32[128,128]{1,0:T(8,128)S(1)} custom-call(f32[128,128]{1,0:T(8,128)S(1)} %fusion.13), custom_call_target="Cholesky" | custom-call | tf_op jit(solution)/shard_map/jit(cholesky)/cholesky | solution.py:12
  562.0 0.6 compare_reduce_fusion
  562.6 0.7 fusion.11
  563.3 9.8 %custom-call.6 = f32[1,128,128]{1,2,0:T(8,128)S(1)} custom-call(f32[1,128,128]{2,1,0:T(8,128)S(1)} %fusion.11), custom_call_target="InvertDiagBlocksLowerTriangular" | custom-call | tf_op jit(solution)/shard_map/triangular_solve | solution.py:13
  573.1 2.2 broadcast_multiply_fusion.1
  575.4 1.0 convolution_bitcast_fusion.1
  576.4 0.0 all-reduce.17.cloned.1.call-start
  576.5 137.4 %all-reduce.15.cloned.1.call-done = f32[128,128]{0,1:T(8,128)} async-done(((f32[128,128]{0,1:T(8,128)}), f32[128,128]{0,1:T(8,128)}) %all-reduce.15.cloned.1.call-update) | async-done | bytes 65552 | tf_op jit(solution)/shard_map/psum | solution.py:41
  713.9 2.2 fusion.18
  716.1 68.0 %all-reduce.17.cloned.1.call-done = f32[128,1664]{1,0:T(8,128)} async-done(((f32[128,1664]{1,0:T(8,128)}), f32[128,1664]{1,0:T(8,128)}) %all-reduce.17.cloned.1.call-update) | async-done | bytes 851984 | tf_op jit(solution)/shard_map/psum | solution.py:48
  784.1 2.1 broadcast_multiply_fusion
  (11 shorter events, 0.1 us)
Async XLA Ops:
  7.2 195.0 %copy-start = (bf16[1664,128]{1,0:T(8,128)(2,1)S(1)}, bf16[1664,128]{1,0:T(8,128)(2,1)}, u32[]{:S(2)}) copy-start(bf16[1664,128]{1,0:T(8,128)(2,1)} %param.9) | copy-start | bytes 1277956
  7.2 86.4 %all-gather.2.cloned.1.call-start = ((), (), s32[]{:S(2)}) async-start(), calls=%async_computation | async-start | bytes 4325376 | tf_op jit(solution)/shard_map/all_gather | solution.py:19
  7.9 192.9 %all-reduce.7.cloned.1.call-start = ((), (), s32[]{:S(2)}) async-start(), calls=%async_computation.1 | async-start | bytes 13631488 | tf_op jit(solution)/shard_map/psum | solution.py:26
  106.9 93.9 %copy-start.2 = (bf16[128,1664]{1,0:T(8,128)(2,1)S(1)}, bf16[128,1664]{1,0:T(8,128)(2,1)}, u32[]{:S(2)}) copy-start(bf16[128,1664]{1,0:T(8,128)(2,1)} %param.7) | copy-start | bytes 1277956
  106.9 233.1 %copy-start.1 = (bf16[128,512]{1,0:T(8,128)(2,1)S(1)}, bf16[128,512]{1,0:T(8,128)(2,1)}, u32[]{:S(2)}) copy-start(bf16[128,512]{1,0:T(8,128)(2,1)} %param.8) | copy-start | bytes 393220
  107.0 233.1 %all-reduce.9.cloned.1.call-start = ((), (), s32[]{:S(2)}) async-start(), calls=%async_computation.2 | async-start | bytes 131072 | tf_op jit(solution)/shard_map/psum | solution.py:30
  203.1 204.8 %all-reduce.11.cloned.1.call-start = ((), (), s32[]{:S(2)}) async-start(), calls=%async_computation.3 | async-start | bytes 524288 | tf_op jit(solution)/shard_map/psum | solution.py:35
  341.9 206.5 %all-reduce.13.cloned.1.call-start = ((), (), s32[]{:S(2)}) async-start(), calls=%async_computation.4 | async-start | bytes 131072 | tf_op jit(solution)/shard_map/psum | solution.py:37
  410.0 303.9 %all-reduce.15.cloned.1.call-start = ((), (), s32[]{:S(2)}) async-start(), calls=%async_computation.5 | async-start | bytes 131072 | tf_op jit(solution)/shard_map/psum | solution.py:41
  576.4 207.7 %all-reduce.17.cloned.1.call-start = ((), (), s32[]{:S(2)}) async-start(), calls=%async_computation.6 | async-start | bytes 1703936 | tf_op jit(solution)/shard_map/psum | solution.py:48
Sparse Core Ops, SparseCore 0:
  10.6 82.9 all-gather.1
  107.1 93.6 all-reduce.6
  204.8 135.1 all-reduce.8
  342.8 65.1 all-reduce.10
  412.2 136.2 all-reduce.12
  576.5 137.2 all-reduce.14
  716.9 67.1 all-reduce.16
where the time goes:
time: 795 us; the launch traced here: 793 us
  waiting for transfers between devices  727 us (91%)
  other arithmetic  27.2 us (3%)
  matrix products  23.6 us (3%)
  between operations  14.2 us (2%)
    psum x1, waiting for transfers between devices, shards(): gram = lax.psum(gram_local, 'tensor')  138 us
    psum x1, waiting for transfers between devices, shards(): coeff = lax.psum(coeff_part, 'tensor')  137 us
    psum x1, waiting for transfers between devices, shards(): sketch = lax.psum(sketch_part, 'tensor')  137 us
    psum x1, waiting for transfers between devices, shards(): summed = lax.psum(partial_all, 'dp')  93.8 us
    all_gather x1, waiting for transfers between devices, shards(): gathered = lax.all_gather(out_grad, 'tensor', axis=0, tiled=True)  85.6 us
    psum x1, waiting for transfers between devices, shards(): corange = lax.psum(corange_part, 'dp') * factor  68 us
    psum x1, waiting for transfers between devices, shards(): range_cols = lax.psum(range_part, 'dp') * factor  66 us
  transfers between devices with their start and end apart: 7, of which 7 were waited for; matrix products, arithmetic and copies ran while one was open for 0% of the time, Pallas kernels for 0%

commit v1 on v0

v1 whole, which is shorter than its diff:
```python
import functools
import math

import jax
import jax.numpy as jnp
from jax import lax
from jax.experimental import pallas as pl
from jax.experimental.pallas import tpu as pltpu
from jax.sharding import PartitionSpec as P

MESH = pl.DeviceIdType.MESH
F32 = jnp.float32
BF16 = jnp.bfloat16

NX, NC, NY, NZ = 4, 2, 4, 8
CUT = 896
LAST = 2 * (NZ // 2) - 1


def slot_from_below(k):
    return LAST if k == NZ // 2 else 2 * k


def slot_from_above(k):
    return LAST if k == NZ // 2 else 2 * k - 1


OFFSET = {0: 0, LAST: NZ // 2}
for _k in range(1, NZ // 2):
    OFFSET[slot_from_below(_k)] = NZ - _k
    OFFSET[slot_from_above(_k)] = _k


def split3(v):
    hi = v.astype(BF16)
    rest = v - hi.astype(F32)
    mid = rest.astype(BF16)
    low = (rest - mid.astype(F32)).astype(BF16)
    return hi, mid, low


def dot(a, b, ca, cb, precision=None):
    return lax.dot_general(
        a, b, (((ca,), (cb,)), ((), ())), preferred_element_type=F32, precision=precision
    )


HIGHEST = lax.Precision.HIGHEST


def inverse_factor(gram, work):
    n = gram.shape[0]
    ri = lax.broadcasted_iota(jnp.int32, (n, n), 0)
    ci = lax.broadcasted_iota(jnp.int32, (n, n), 1)
    work[:, :n] = gram
    work[:, n:] = jnp.where(ri == ci, 1.0, 0.0).astype(F32)
    sub = lax.broadcasted_iota(jnp.int32, (8, n), 0)
    sub2 = lax.broadcasted_iota(jnp.int32, (8, 2 * n), 0)
    for b in range(n // 8):
        rows = slice(8 * b, 8 * b + 8)
        panel = work[rows, :]
        cols = [
            jnp.broadcast_to(panel[:, 8 * b + m : 8 * b + m + 1], (8, n)) for m in range(8)
        ]
        for k in range(8):
            inv = lax.rsqrt(cols[k][k : k + 1, :])
            fac = jnp.where(sub > k, cols[k] * inv, 0.0)
            fac2 = jnp.concatenate([fac, fac], axis=1)
            inv2 = jnp.concatenate([inv, inv], axis=1)
            row = panel[k : k + 1, :] * inv2
            panel = jnp.where(sub2 == k, row, panel - fac2 * row)
            for m in range(k + 1, 8):
                cols[m] = cols[m] - fac * (cols[m][k : k + 1, :] * inv)
        work[rows, :] = panel
        done = 8 * (b + 1)
        if done < n:
            hi = panel.astype(BF16).astype(F32)
            mid = (panel - hi).astype(BF16).astype(F32)
            low = panel - hi - mid
            left = jnp.concatenate([hi, hi, mid, hi, low, mid], axis=0)[:, :n].astype(BF16)
            right = jnp.concatenate([hi, mid, hi, low, hi, mid], axis=0).astype(BF16)
            work[done:, :] = work[done:, :] - dot(left, right, 0, 0)[done:, :]


def kernel(
    og, dw, gate, inp, test, basis, corange,
    G, W, GT, XB, TM, SIL, PT, SIBR, SIB0, HG, FS, FR, XS, RX, U, XT,
    SP, S1, S2, SF, V, V1, V2, VF, WK, M, MS, MC, MR, MF,
    sends, recvs, local,
):
    d, t = lax.axis_index("dp"), lax.axis_index("tensor")
    x, c = d // NC, lax.rem(d, NC)
    y, z = t // NZ, lax.rem(t, NZ)
    tokens = NX * NC * XB.shape[1]
    factor = 1.0 / math.sqrt(tokens)
    features = inp.shape[1] * NY * NZ

    def mod(a, n):
        return lax.rem(a + n, n)

    def at_yz(yy, zz):
        return {"dp": d, "tensor": yy * NZ + zz}

    def at_xc(xx, cc):
        return {"dp": xx * NC + cc, "tensor": t}

    zu, zd = at_yz(y, mod(z + 1, NZ)), at_yz(y, mod(z - 1, NZ))
    yu, yd, y2 = at_yz(mod(y + 1, NY), z), at_yz(mod(y - 1, NY), z), at_yz(mod(y + 2, NY), z)
    xu, xd = mod(x + 1, NX), mod(x - 1, NX)
    twin = at_xc(x, 1 - c)

    pending = []
    count = {"s": 0, "r": 0}

    def take_recv(n):
        base = count["r"]
        count["r"] += n
        return base

    def send(src, dst, recv, dev, when=None):
        idx = count["s"]
        count["s"] += 1
        cp = pltpu.make_async_remote_copy(
            src_ref=src, dst_ref=dst, send_sem=sends.at[idx], recv_sem=recvs.at[recv],
            device_id=dev, device_id_type=MESH,
        )
        if when is None:
            cp.start()
        else:
            pl.when(when)(cp.start)
        pending.append((cp, when))

    def arrive(ref, recv):
        pltpu.make_async_remote_copy(
            src_ref=ref, dst_ref=ref, send_sem=sends.at[0], recv_sem=recvs.at[recv],
            device_id=twin, device_id_type=MESH,
        ).wait_recv()

    q0, qp, qn, q2 = mod(y - x, NY), mod(y - 1 - x, NY), mod(y + 1 - x, NY), mod(y + 2 - x, NY)

    half = og.shape[0] // 2
    loads = [
        pltpu.make_async_copy(og.at[pl.ds(0, half)], G.at[q0 * 2], local.at[0]),
        pltpu.make_async_copy(og.at[pl.ds(half, half)], G.at[q0 * 2 + 1], local.at[1]),
        pltpu.make_async_copy(inp, XB.at[d], local.at[2]),
        pltpu.make_async_copy(dw, W, local.at[3]),
        pltpu.make_async_copy(gate, GT, local.at[4]),
        pltpu.make_async_copy(test, TM, local.at[5]),
    ]
    for cp in loads:
        cp.start()

    barrier = pltpu.get_barrier_semaphore()
    peers = [at_yz(y, mod(z + o, NZ)) for o in range(1, NZ)]
    peers += [yu, yd, y2]
    peers += [at_xc(mod(x + o, NX), cc) for o in range(1, NX) for cc in range(NC)] + [twin]
    for dev in peers:
        pl.semaphore_signal(barrier, inc=1, device_id=dev, device_id_type=MESH)
    pl.semaphore_wait(barrier, len(peers))
    loads[0].wait()
    loads[1].wait()

    ag = take_recv(8 * NY * 2)

    def item(slot, q, h):
        return (slot * NY + q) * 2 + h

    def pass_on(slot, q, h, to_slot, dev, when=None):
        send(G.at[item(slot, q, h)], G.at[item(to_slot, q, h)], ag + item(to_slot, q, h), dev, when)

    def got(slot, q, h):
        arrive(G.at[item(slot, q, h)], ag + item(slot, q, h))

    below, above = slot_from_below, slot_from_above
    TOP = NZ // 2

    pass_on(0, q0, 1, 0, yu)
    pass_on(0, q0, 1, 0, yd)
    pass_on(0, q0, 0, below(1), zu)
    pass_on(0, q0, 0, above(1), zd)
    pass_on(0, q0, 1, 0, y2)
    pass_on(0, q0, 0, 0, yu)
    pass_on(0, q0, 0, 0, yd)

    loads[2].wait()
    xr = take_recv(NX * NC)
    for o in (1, 3, 2):
        send(XB.at[d], XB.at[d], xr + d, at_xc(mod(x + o, NX), c))
    send(XB.at[d], XB.at[d], xr + d, twin)

    def first_half_from_z(k):
        if k < TOP:
            s = above(k)
            got(s, q0, 0)
            if k + 1 < TOP:
                pass_on(s, q0, 0, above(k + 1), zd)
            pass_on(s, q0, 0, s, yu)
            pass_on(s, q0, 0, s, yd)
        s = below(k)
        got(s, q0, 0)
        if k < TOP:
            pass_on(s, q0, 0, below(k + 1), zu)
        pass_on(s, q0, 0, s, yu)
        pass_on(s, q0, 0, s, yd)

    def first_half_from_y(s):
        got(s, qp, 0)
        if s % 2 == 0:
            pass_on(s, qp, 0, s, yu)
        got(s, qn, 0)
        if s % 2 == 1:
            pass_on(s, qn, 0, s, yd)

    def on_along_z(q):
        pass_on(0, q, 1, below(1), zu)
        pass_on(0, q, 1, above(1), zd)

    sibs = take_recv(24)
    sib0 = take_recv(4)
    fw = take_recv(16)
    rx = take_recv(16)
    n = W.shape[0]
    WIDE = 256

    def column(s):
        return lax.rem(z + OFFSET[s], NZ)

    def product(s0, slots):
        i0, ni = s0 * NY * 2, slots * NY * 2
        rows = ni * half

        def cols_at(start, width):
            a = G[pl.ds(i0, ni)].reshape(rows, G.shape[2])
            b = W[pl.ds(start, width), :]
            PT[pl.ds(i0, ni), :, pl.ds(start, width)] = dot(a, b, 1, 1).reshape(ni, half, width)

        def body(j, _):
            cols_at(pl.multiple_of(j * WIDE, WIDE), WIDE)
            return 0

        lax.fori_loop(0, n // WIDE, body, 0)
        if n % WIDE:
            cols_at(n - n % WIDE, n % WIDE)

    def exchange(s):
        owner = column(s) // (NZ // NC)
        zc = lax.rem(column(s), NZ // NC)
        for q in range(1, NX):
            send(
                PT.at[item(s, q, 1 - c)], SIBR.at[s, q - 1], sibs + s * 3 + q - 1, twin
            )
        send(PT.at[pl.ds(item(s, 0, 0), 2)], SIB0.at[zc], sib0 + zc, twin, owner != c)

        @pl.when(owner == c)
        def _():
            HG[zc] = PT[pl.ds(item(s, 0, 0), 2)]

    def two_hops(s):
        arrive(SIBR.at[s, 1], sibs + s * 3 + 1)
        FS[s] = (PT[item(s, 2, c)] + SIBR[s, 1]).astype(BF16)
        send(FS.at[s, :, pl.ds(0, CUT)], FR.at[s, :, pl.ds(0, CUT)], fw + 2 * s, at_xc(xu, c))
        send(
            FS.at[s, :, pl.ds(CUT, n - CUT)], FR.at[s, :, pl.ds(CUT, n - CUT)],
            fw + 2 * s + 1, at_xc(xd, c),
        )

    def one_hop(s):
        owner = column(s) // (NZ // NC)
        zc = lax.rem(column(s), NZ // NC)
        arrive(SIBR.at[s, 0], sibs + s * 3)
        arrive(SIBR.at[s, 2], sibs + s * 3 + 2)
        arrive(FR.at[s, :, pl.ds(0, CUT)], fw + 2 * s)
        v = PT[item(s, 1, c)] + SIBR[s, 0]
        XS[s, 0, :, :CUT] = (v[:, :CUT] + FR[s, :, :CUT].astype(F32)).astype(BF16)
        XS[s, 0, :, CUT:] = v[:, CUT:].astype(BF16)
        k = (zc * 2 + c) * 2
        send(XS.at[s, 0], RX.at[0, zc, c], rx + k, at_xc(xu, owner))
        arrive(FR.at[s, :, pl.ds(CUT, n - CUT)], fw + 2 * s + 1)
        v = PT[item(s, 3, c)] + SIBR[s, 2]
        XS[s, 1, :, :CUT] = v[:, :CUT].astype(BF16)
        XS[s, 1, :, CUT:] = (v[:, CUT:] + FR[s, :, CUT:].astype(F32)).astype(BF16)
        send(XS.at[s, 1], RX.at[1, zc, c], rx + k + 1, at_xc(xd, owner))

    groups = [[0]] + [[above(k), below(k)] for k in range(1, TOP)] + [[LAST]]

    first_half_from_z(1)
    on_along_z(q0)
    for q in (qp, qn, q2):
        got(0, q, 1)
        on_along_z(q)
    first_half_from_y(0)
    got(0, q2, 0)
    loads[3].wait()
    product(0, 1)
    for s in groups[0]:
        exchange(s)
    for k in range(1, TOP + 1):
        if k < TOP:
            first_half_from_z(k + 1)
            for q in range(NY):
                got(above(k), q, 1)
                if k + 1 < TOP or q >= 2:
                    pass_on(above(k), q, 1, above(k + 1), zd)
                got(below(k), q, 1)
                if k + 1 < TOP or q < 2:
                    pass_on(below(k), q, 1, below(k + 1), zu)
        else:
            for q in range(NY):
                got(LAST, q, 1)
        if k == 1:
            loads[4].wait()
            g = GT[...].astype(F32)
            SIL[...] = g * (1.0 / (1.0 + jnp.exp(-g)))
            for o in (1, 3, 2):
                e = mod(x + o, NX) * NC + c
                arrive(XB.at[e], xr + e)
                send(XB.at[e], XB.at[e], xr + e, twin)
        if k == 2:
            for o in range(NX):
                e = mod(x + o, NX) * NC + 1 - c
                arrive(XB.at[e], xr + e)
            rows = XB.shape[1]
            for e in range(NX * NC):
                XT[:, e * rows : (e + 1) * rows] = XB[e].T
        for s in groups[k]:
            first_half_from_y(s)
        for s in groups[k]:
            got(s, q2, 0)
        product(groups[k][0], len(groups[k]))
        for s in groups[k]:
            exchange(s)
        for s in groups[k - 1]:
            two_hops(s)
        if k >= 2:
            for s in groups[k - 2]:
                one_hop(s)
    for s in groups[TOP]:
        two_hops(s)
    for s in groups[TOP - 1]:
        one_hop(s)
    for s in groups[TOP]:
        one_hop(s)

    loads[5].wait()
    for zc in range(NZ // NC):
        arrive(SIB0.at[zc], sib0 + zc)
        for h in range(2):
            arrive(RX.at[0, zc, h], rx + (zc * 2 + h) * 2)
            arrive(RX.at[1, zc, h], rx + (zc * 2 + h) * 2 + 1)
            v = (HG[zc, h] + SIB0[zc, h]) + (
                RX[0, zc, h].astype(F32) + RX[1, zc, h].astype(F32)
            )
            rows = slice((zc * 2 + h) * half, (zc * 2 + h + 1) * half)
            U[rows, :] = (v * SIL[rows, :]).astype(BF16)

    r = TM.shape[1]
    part = r // NZ
    own = XB.shape[1]

    def over_tensor(src, first, second, full, place):
        r1, r2, r3 = take_recv(NZ), take_recv(NY), take_recv(NZ)
        first[z] = src[z]
        for o in (4, 3, 5, 2, 6, 1, 7):
            zz = mod(z + o, NZ)
            send(src.at[zz], first.at[z], r1 + z, at_yz(y, zz))
        for o in (1, 7, 2, 6, 3, 5, 4):
            zz = mod(z + o, NZ)
            arrive(first.at[zz], r1 + zz)
        v = first[0]
        for j in range(1, NZ):
            v = v + first[j]
        second[y] = v
        for o in (2, 1, 3):
            send(second.at[y], second.at[y], r2 + y, at_yz(mod(y + o, NY), z))
        for o in (1, 3, 2):
            yy = mod(y + o, NY)
            arrive(second.at[yy], r2 + yy)
        v = second[0]
        for j in range(1, NY):
            v = v + second[j]
        place(z, v)
        for o in (4, 3, 5, 2, 6, 1, 7):
            send(full(z), full(z), r3 + z, at_yz(y, mod(z + o, NZ)))
        for o in (1, 7, 2, 6, 3, 5, 4):
            zz = mod(z + o, NZ)
            arrive(full(zz), r3 + zz)

    def over_dp(full):
        r1 = take_recv(NX * NC)
        for o in (2, 1, 3):
            send(full(d), full(d), r1 + d, at_xc(mod(x + o, NX), c))
        send(full(d), full(d), r1 + d, twin)
        for o in (1, 3, 2):
            e = mod(x + o, NX) * NC + c
            arrive(full(e), r1 + e)
            send(full(e), full(e), r1 + e, twin)
        for o in range(NX):
            e = mod(x + o, NX) * NC + 1 - c
            arrive(full(e), r1 + e)

    SP[...] = dot(U[...], TM[...], 1, 0).reshape(NZ, part, r)

    def place_s(zz, v):
        SF[d, zz] = v

    over_tensor(SP, S1, S2, lambda zz: SF.at[d, zz], place_s)
    over_dp(lambda e: SF.at[e])

    s = SF[...].reshape(tokens, r)
    rc = jnp.zeros((XT.shape[0], r), F32)
    xt = XT[...]
    for piece in split3(s)[::-1]:
        rc = rc + dot(xt, piece, 1, 0)
    rc = rc * factor
    V[:, 0] = dot(rc, rc, 0, 0, HIGHEST).reshape(NZ, part, r)
    co = jnp.zeros((own, r), F32)
    xown = XB[d]
    for piece in split3(rc)[::-1]:
        co = co + dot(xown, piece, 1, 0)
    V[:, 1] = co.reshape(NZ, part, r)

    def place_v(zz, v):
        VF[zz] = v

    over_tensor(V, V1, V2, lambda zz: VF.at[zz], place_v)

    tt = VF[:, 1].reshape(own, r)
    mm = jnp.zeros((r, n), F32)
    for piece in split3(tt)[::-1]:
        mm = mm + dot(piece, U[...], 0, 0)
    M[...] = mm.reshape(NX, NC, r // (NX * NC), n)
    m1, m2 = take_recv(NX), take_recv(NX)
    for o in (2, 1, 3, 0):
        e = mod(x + o, NX)
        send(M.at[e, 1 - c], MS.at[e], m1 + e, twin)
    for o in (2, 1, 3, 0):
        e = mod(x + o, NX)
        arrive(MS.at[e], m1 + e)
        MC[e] = M[e, c] + MS[e]
        if o:
            send(MC.at[e], MR.at[x], m2 + x, at_xc(e, c))
    MR[x] = MC[x]

    inverse_factor(VF[:, 0].reshape(r, r), WK)

    for o in (1, 3, 2):
        e = mod(x + o, NX)
        arrive(MR.at[e], m2 + e)
    v = MR[0]
    for j in range(1, NX):
        v = v + MR[j]
    MF[d] = v
    inv = WK[:, r:]
    basis[...] = dot(rc, inv, 1, 1, HIGHEST) * math.sqrt(features)
    over_dp(lambda e: MF.at[e])
    corange[...] = dot(inv, MF[...].reshape(r, n), 1, 0, HIGHEST) * factor

    assert count["s"] <= 220 and count["r"] <= 230, count
    for cp, when in pending:
        if when is None:
            cp.wait_send()
        else:
            pl.when(when)(cp.wait_send)


def shards(out_grad, down_weight, gate_pre, inputs, test_matrix):
    rows, depth = out_grad.shape
    n = down_weight.shape[0]
    own, width = inputs.shape
    r = test_matrix.shape[1]
    half = rows // 2
    part = r // NZ
    dp = NX * NC
    vm = pltpu.VMEM
    scratch = [
        vm((8 * NY * 2, half, depth), BF16),
        vm((n, depth), BF16),
        vm((own, n), BF16),
        vm((dp, own, width), BF16),
        vm((n, r), BF16),
        vm((own, n), F32),
        vm((8 * NY * 2, half, n), F32),
        vm((8, 3, half, n), F32),
        vm((NZ // NC, 2, half, n), F32),
        vm((NZ // NC, 2, half, n), F32),
        vm((8, half, n), BF16),
        vm((8, half, n), BF16),
        vm((8, 2, half, n), BF16),
        vm((2, NZ // NC, 2, half, n), BF16),
        vm((own, n), BF16),
        vm((width, dp * own), BF16),
        vm((NZ, part, r), F32),
        vm((NZ, part, r), F32),
        vm((NY, part, r), F32),
        vm((dp, NZ, part, r), F32),
        vm((NZ, 2, part, r), F32),
        vm((NZ, 2, part, r), F32),
        vm((NY, 2, part, r), F32),
        vm((NZ, 2, part, r), F32),
        vm((r, 2 * r), F32),
        vm((NX, NC, r // dp, n), F32),
        vm((NX, r // dp, n), F32),
        vm((NX, r // dp, n), F32),
        vm((NX, r // dp, n), F32),
        vm((dp, r // dp, n), F32),
        pltpu.SemaphoreType.DMA((220,)),
        pltpu.SemaphoreType.DMA((230,)),
        pltpu.SemaphoreType.DMA((6,)),
    ]
    flops = 2 * dp * own * n * depth
    return pl.pallas_call(
        kernel,
        out_shape=(
            jax.ShapeDtypeStruct((width, r), F32),
            jax.ShapeDtypeStruct((r, n), F32),
        ),
        in_specs=[pl.BlockSpec(memory_space=pl.ANY)] * 5,
        out_specs=[pl.BlockSpec(memory_space=pltpu.VMEM)] * 2,
        scratch_shapes=scratch,
        cost_estimate=pl.CostEstimate(
            flops=flops, bytes_accessed=2 * n * depth, transcendentals=own * n
        ),
        compiler_params=pltpu.CompilerParams(
            collective_id=0, has_side_effects=True, vmem_limit_bytes=60 * 1024 * 1024
        ),
    )(out_grad, down_weight, gate_pre, inputs, test_matrix)


def solution(mesh):
    return jax.shard_map(
        shards,
        mesh=mesh,
        in_specs=(
            P("tensor", "dp"),
            P("tensor", "dp"),
            P("dp", "tensor"),
            P("dp", "tensor"),
            P("tensor", None),
        ),
        out_specs=(P("tensor", None), P(None, "tensor")),
        check_vma=False,
    )
```

time: 795 us -> 129 us (0.16)
  waiting for transfers between devices: 727 us -> 0 us
  Pallas kernels: 0 us -> 124 us
  other arithmetic: 27.2 us -> 0 us
  matrix products: 23.6 us -> 0 us
  between operations: 14.2 us -> 0.64 us
    psum x6 -> x0, waiting for transfers between devices: 640 us -> none  [the longest x1 138 us: shards(): gram = lax.psum(gram_local, 'tensor')]
    pallas_call x0 -> x1, Pallas kernels: none -> 124 us  [shards(): pl.pallas_call(kernel, out_shape=(jax.ShapeDtypeStruct((width, r), F32),...]
    all_gather x1 -> x0, waiting for transfers between devices: 85.6 us -> none  [shards(): gathered = lax.all_gather(out_grad, 'tensor', axis=0, tiled=True)]
    another operation x5 -> x0, other arithmetic: 22.9 us -> none  [the longest x3 12.4 us: orthonormal(): lower = jnp.linalg.cholesky(gram)]
    dot_general x6 -> x0, matrix products: 21.4 us -> none  [the longest x1 13.3 us: shards(): lax.dot_general(gathered, down_weight, (((1,), (1,)), ((), ())), preferre...]
  transfers between devices with their start and end apart: 7 -> 0, of which waited for: 7 -> 0; matrix products, arithmetic and copies ran while one was open for 0% -> 0% of each run, Pallas kernels for 0% -> 0%
where the time goes in v1:
time: 129 us
  Pallas kernels  124 us (96%)
  local copies, waits for them, and re-layouts  3.78 us (3%)
    pallas_call x1, Pallas kernels, shards(): pl.pallas_call(kernel, out_shape=(jax.ShapeDtypeStruct((width, r), F32),...  124 us
    unnamed x2, local copies, waits for them, and re-layouts  3.78 us

profile of v1, /device:TPU:1, one launch (start us, length us, event | category | flops | bytes accessed | tf_op | source)
XLA Modules:
  0.0 128.6 jit_solution(17359907141107004447)
XLA Ops:
  0.6 124.2 %shard_map.68 = (f32[512,128]{1,0:T(8,128)}, f32[128,1664]{1,0:T(8,128)}) custom-call(bf16[32,2048]{1,0:T(8,128)(2,1)} %og.1, bf16[1664,2048]{1,0:T(8,128)(2,1)} %dw.1, bf16[128,1664]{1,0:T(8,128)(2,1)} %gate.1, bf16[128,512]{1,0:T(8,128)(2,1)} %inp.1, bf16[1664,128]{1,0:T(8,128)(2,1)} %test.1), custom_call_target="tpu_custom_call" | custom-call | flops 6979321856 | bytes 6815744 | tf_op jit(solution)/shard_map/pallas_call | solution.py:511
  124.8 1.7 %copy.9 = f32[512,128]{1,0:T(8,128)} copy(f32[512,128]{1,0:T(8,128)} %get-tuple-element.4) | data formatting | bytes 524288
  126.5 2.1 %copy.10 = f32[128,1664]{1,0:T(8,128)} copy(f32[128,1664]{1,0:T(8,128)} %get-tuple-element.5) | data formatting | bytes 1703936

commit v2 on v1

v2 whole, which is shorter than its diff:
```python
import functools
import math

import jax
import jax.numpy as jnp
from jax import lax
from jax.experimental import pallas as pl
from jax.experimental.pallas import tpu as pltpu
from jax.sharding import PartitionSpec as P

MESH = pl.DeviceIdType.MESH
F32 = jnp.float32
BF16 = jnp.bfloat16

NX, NC, NY, NZ = 4, 2, 4, 8
CUT = 1024
LAST = 2 * (NZ // 2) - 1


def slot_from_below(k):
    return LAST if k == NZ // 2 else 2 * k


def slot_from_above(k):
    return LAST if k == NZ // 2 else 2 * k - 1


OFFSET = {0: 0, LAST: NZ // 2}
STEP = {0: 0, LAST: NZ // 2}
for _k in range(1, NZ // 2):
    OFFSET[slot_from_below(_k)] = NZ - _k
    OFFSET[slot_from_above(_k)] = _k
    STEP[slot_from_below(_k)] = STEP[slot_from_above(_k)] = _k

ARRIVALS = [
        (2, 0, 0), (1, 0, 0), (0, 3, 1), (0, 1, 1), (2, 0, 1), (1, 0, 1), (0, 3, 0),
        (0, 1, 0), (0, 2, 1), (4, 0, 0), (3, 0, 0), (2, 3, 0), (2, 1, 0), (2, 3, 1),
        (1, 3, 1), (1, 3, 0), (1, 1, 0), (2, 1, 1), (1, 1, 1), (0, 2, 0), (4, 1, 0),
        (4, 0, 1), (3, 0, 1), (4, 3, 0), (3, 1, 0), (2, 2, 1), (1, 2, 1), (3, 3, 0),
        (1, 2, 0), (6, 0, 0), (5, 0, 0), (2, 2, 0), (4, 3, 1), (3, 3, 1), (4, 2, 0),
        (3, 2, 0), (4, 1, 1), (3, 1, 1), (6, 3, 0), (6, 1, 0), (6, 0, 1), (5, 0, 1),
        (5, 3, 0), (5, 1, 0), (4, 2, 1), (3, 2, 1), (7, 0, 0), (5, 3, 1), (6, 2, 0),
        (6, 3, 1), (5, 1, 1), (5, 2, 0), (6, 1, 1), (5, 2, 1), (7, 3, 0), (7, 1, 0),
        (7, 0, 1), (7, 3, 1), (6, 2, 1), (7, 2, 1), (7, 1, 1), (7, 2, 0),
]
HALF_TURN = {0: True, 1: True, 3: False, 2: False}


def split3(v):
    hi = v.astype(BF16)
    rest = v - hi.astype(F32)
    mid = rest.astype(BF16)
    low = (rest - mid.astype(F32)).astype(BF16)
    return hi, mid, low


def dot(a, b, ca, cb, precision=None):
    return lax.dot_general(
        a, b, (((ca,), (cb,)), ((), ())), preferred_element_type=F32, precision=precision
    )


HIGHEST = lax.Precision.HIGHEST


def inverse_factor(gram, work, midway):
    n = gram.shape[0]
    ri = lax.broadcasted_iota(jnp.int32, (n, n), 0)
    ci = lax.broadcasted_iota(jnp.int32, (n, n), 1)
    work[:, :n] = gram
    work[:, n:] = jnp.where(ri == ci, 1.0, 0.0).astype(F32)
    sub = lax.broadcasted_iota(jnp.int32, (8, n), 0)
    sub2 = lax.broadcasted_iota(jnp.int32, (8, 2 * n), 0)
    for b in range(n // 8):
        if b == n // 16:
            midway()
        rows = slice(8 * b, 8 * b + 8)
        panel = work[rows, :]
        cols = [
            jnp.broadcast_to(panel[:, 8 * b + m : 8 * b + m + 1], (8, n)) for m in range(8)
        ]
        for k in range(8):
            inv = lax.rsqrt(cols[k][k : k + 1, :])
            fac = jnp.where(sub > k, cols[k] * inv, 0.0)
            fac2 = jnp.concatenate([fac, fac], axis=1)
            inv2 = jnp.concatenate([inv, inv], axis=1)
            row = panel[k : k + 1, :] * inv2
            panel = jnp.where(sub2 == k, row, panel - fac2 * row)
            for m in range(k + 1, 8):
                cols[m] = cols[m] - fac * (cols[m][k : k + 1, :] * inv)
        work[rows, :] = panel
        done = 8 * (b + 1)
        if done < n:
            hi = panel.astype(BF16).astype(F32)
            mid = (panel - hi).astype(BF16).astype(F32)
            low = panel - hi - mid
            left = jnp.concatenate([hi, hi, mid, hi, low, mid], axis=0)[:, :n].astype(BF16)
            right = jnp.concatenate([hi, mid, hi, low, hi, mid], axis=0).astype(BF16)
            work[done:, :] = work[done:, :] - dot(left, right, 0, 0)[done:, :]


def kernel(
    og, dw, gate, inp, test, basis, corange,
    GA, GB, W, GT, XB, TM, SIL, PT, SIBR, SIB0, HG, XS, RX, UF, XT,
    SP, S1, S2, SF, RC, V, V1, V2, GF, TF, WK,
    sends, recvs, local,
):
    d, t = lax.axis_index("dp"), lax.axis_index("tensor")
    x, c = d // NC, lax.rem(d, NC)
    y, z = t // NZ, lax.rem(t, NZ)
    tokens = NX * NC * XB.shape[1]
    factor = 1.0 / math.sqrt(tokens)
    features = inp.shape[1] * NY * NZ

    def mod(a, n):
        return lax.rem(a + n, n)

    def at_yz(yy, zz):
        return {"dp": d, "tensor": yy * NZ + zz}

    def at_xc(xx, cc):
        return {"dp": xx * NC + cc, "tensor": t}

    def around(o, p):
        return {"dp": mod(x + o, NX) * NC + c, "tensor": y * NZ + mod(z + p, NZ)}

    zu, zd = at_yz(y, mod(z + 1, NZ)), at_yz(y, mod(z - 1, NZ))
    yu, yd, y2 = at_yz(mod(y + 1, NY), z), at_yz(mod(y - 1, NY), z), at_yz(mod(y + 2, NY), z)
    xu, xd = mod(x + 1, NX), mod(x - 1, NX)
    twin = at_xc(x, 1 - c)

    pending = []
    count = {"s": 0, "r": 0}

    def finish():
        assert count["s"] <= 280 and count["r"] <= 280, count
        for make, when in pending:
            if when is None:
                make().wait_send()
            else:
                pl.when(when)(make().wait_send)

    def take_recv(n):
        base = count["r"]
        count["r"] += n
        return base

    def send(src, dst, recv, dev, when=None):
        idx = count["s"]
        count["s"] += 1

        def make():
            return pltpu.make_async_remote_copy(
                src_ref=src() if callable(src) else src,
                dst_ref=dst() if callable(dst) else dst,
                send_sem=sends.at[idx], recv_sem=recvs.at[recv() if callable(recv) else recv],
                device_id=dev, device_id_type=MESH,
            )

        if when is None:
            make().start()
        else:
            pl.when(when)(make().start)
        pending.append((make, when))

    def arrive(ref, recv):
        pltpu.make_async_remote_copy(
            src_ref=ref, dst_ref=ref, send_sem=sends.at[0], recv_sem=recvs.at[recv],
            device_id=twin, device_id_type=MESH,
        ).wait_recv()

    q0, qp, qn, q2 = mod(y - x, NY), mod(y - 1 - x, NY), mod(y + 1 - x, NY), mod(y + 2 - x, NY)

    half = og.shape[0] // 2
    loads = [
        pltpu.make_async_copy(og.at[:, pl.ds(0, CUT)], GA.at[q0], local.at[0]),
        pltpu.make_async_copy(
            og.at[:, pl.ds(CUT, og.shape[1] - CUT)], GB.at[q0], local.at[5]
        ),
        pltpu.make_async_copy(inp, XB.at[d], local.at[1]),
        pltpu.make_async_copy(gate, GT, local.at[3]),
        pltpu.make_async_copy(dw, W, local.at[2]),
        pltpu.make_async_copy(test, TM, local.at[4]),
    ]
    for cp in loads:
        cp.start()

    barrier = pltpu.get_barrier_semaphore()
    peers = [zu, zd, yu, yd, y2] + [around(o, 0) for o in range(1, NX)] + [twin]
    for dev in peers:
        pl.semaphore_signal(barrier, inc=1, device_id=dev, device_id_type=MESH)
    pl.semaphore_wait(barrier, len(peers))
    loads[0].wait()
    loads[1].wait()

    ag = take_recv(8 * NY * 2)

    def item(slot, q, h):
        return (GB if h else GA).at[slot * NY + q]

    def mark(slot, q, h):
        return ag + (slot * NY + q) * 2 + h

    def pass_on(slot, q, h, to_slot, dev):
        send(
            lambda: item(slot, q, h), lambda: item(to_slot, q, h),
            lambda: mark(to_slot, q, h), dev
        )

    def got(slot, q, h):
        arrive(item(slot, q, h), mark(slot, q, h))

    below, above = slot_from_below, slot_from_above
    TOP = NZ // 2

    pass_on(0, q0, 0, below(1), zu)
    pass_on(0, q0, 0, above(1), zd)
    pass_on(0, q0, 1, 0, yu)
    pass_on(0, q0, 1, 0, yd)
    pass_on(0, q0, 1, below(1), zu)
    pass_on(0, q0, 1, above(1), zd)
    pass_on(0, q0, 0, 0, yu)
    pass_on(0, q0, 0, 0, yd)
    pass_on(0, q0, 1, 0, y2)

    loads[2].wait()
    xr = take_recv(NX * NC)
    for o in (1, 3, 2):
        send(XB.at[d], XB.at[d], xr + d, at_xc(mod(x + o, NX), c))
    send(XB.at[d], XB.at[d], xr + d, twin)

    row = [q0, qn, q2, qp]

    def arrival(slot, b, h):
        q, k, up = row[b], STEP[slot], slot % 2 == 0
        got(slot, q, h)
        if h:
            if slot == 0:
                pass_on(0, q, 1, below(1), zu)
                pass_on(0, q, 1, above(1), zd)
            elif slot != LAST and (k + 1 < TOP or HALF_TURN[b] == up):
                if up:
                    pass_on(slot, q, 1, below(k + 1), zu)
                else:
                    pass_on(slot, q, 1, above(k + 1), zd)
        elif b == 0:
            if slot != LAST:
                if up:
                    pass_on(slot, q, 0, below(k + 1), zu)
                elif k + 1 < TOP:
                    pass_on(slot, q, 0, above(k + 1), zd)
            pass_on(slot, q, 0, slot, yu)
            pass_on(slot, q, 0, slot, yd)
        elif b == 3 and up:
            pass_on(slot, q, 0, slot, yu)
        elif b == 1 and not up:
            pass_on(slot, q, 0, slot, yd)

    sibs = take_recv(NZ)
    sib0 = take_recv(NZ // NC * 2)
    rx = take_recv(3 * (NZ // NC) * 2)
    n = W.shape[0]
    WIDE = 256

    def column(s):
        return lax.rem(z + OFFSET[s], NZ)

    def owner_of(s):
        return column(s) // (NZ // NC), lax.rem(column(s), NZ // NC)

    def product(s0, slots, events):
        rows = slots * NY * 2 * half

        def cols_at(start, width):
            blocks = pl.ds(s0 * NY, slots * NY)
            a = jnp.concatenate(
                [g[blocks].reshape(rows, g.shape[2]) for g in (GA, GB)], axis=1
            )
            b = W[pl.ds(start, width), :]
            v = dot(a, b, 1, 1).reshape(slots, NY, 2, half, width)
            for h in range(2):
                PT[pl.ds(s0, slots), h, :, :, pl.ds(start, width)] = v[:, :, h]

        def body(j, _):
            cols_at(pl.multiple_of(j * WIDE, WIDE), WIDE)
            for i, todo in enumerate(events):
                if todo:

                    @pl.when(j == i)
                    def _():
                        for act in todo:
                            act()

            return 0

        assert len(events) <= n // WIDE
        lax.fori_loop(0, n // WIDE, body, 0)
        if n % WIDE:
            cols_at(n - n % WIDE, n % WIDE)

    def exchange(s):
        core, zc = owner_of(s)
        send(
            lambda: PT.at[s, 1 - c, pl.ds(1, NX - 1)], lambda: SIBR.at[s], sibs + s, twin
        )
        for h in range(2):
            send(
                lambda h=h: PT.at[s, h, 0], lambda h=h: SIB0.at[zc, h], sib0 + zc * 2 + h,
                twin, core != c,
            )

        @pl.when(core == c)
        def _():
            HG[zc] = PT[s, :, 0]

    owners = [owner_of(s) for s in range(NZ)]
    targets = [[at_xc(mod(x + o, NX), owners[s][0]) for o in range(1, NX)] for s in range(NZ)]
    marks = [
        [rx + ((o - 1) * (NZ // NC) + owners[s][1]) * 2 + c for o in range(1, NX)]
        for s in range(NZ)
    ]

    def outward(s):
        zc = owners[s][1]
        arrive(SIBR.at[s], sibs + s)
        XS[s] = (PT[s, c, 1:] + SIBR[s]).astype(BF16)
        for o in (2, 1, 3):
            send(
                lambda o=o: XS.at[s, o - 1], lambda o=o: RX.at[o - 1, zc, c],
                marks[s][o - 1], targets[s][o - 1],
            )

    def own(s):
        core, zc = owners[s]

        @pl.when(core == c)
        def _():
            for h in range(2):
                arrive(SIB0.at[zc, h], sib0 + zc * 2 + h)
            v = HG[zc] + SIB0[zc]
            for o in range(1, NX):
                for h in range(2):
                    arrive(
                        RX.at[o - 1, zc, h], rx + ((o - 1) * (NZ // NC) + zc) * 2 + h
                    )
                v = v + RX[o - 1, zc].astype(F32)
            UF[d, zc] = (v * SIL[zc].reshape(2, half, n)).astype(BF16)

    groups = [[0]] + [[above(k), below(k)] for k in range(1, TOP)] + [[LAST]]
    ends = [
        1 + max(i for i, a in enumerate(ARRIVALS) if a[0] in g) for g in groups
    ]

    def to_other_core():
        for o in (1, 3, 2):
            e = mod(x + o, NX) * NC + c
            arrive(XB.at[e], xr + e)
            send(XB.at[e], XB.at[e], xr + e, twin)

    def transposed():
        rows = XB.shape[1]
        for o in range(NX):
            e = mod(x + o, NX) * NC + 1 - c
            arrive(XB.at[e], xr + e)
        for e in range(NX * NC):
            XT[:, e * rows : (e + 1) * rows] = XB[e].T

    loads[3].wait()
    g = GT[...].astype(F32)
    SIL[...] = (g * (1.0 / (1.0 + jnp.exp(-g)))).reshape(SIL.shape)
    for a in ARRIVALS[: ends[0]]:
        arrival(*a)
    loads[4].wait()
    turns = n // WIDE
    for k in range(TOP + 1):
        todo = ARRIVALS[ends[k] : ends[k + 1]] if k < TOP else []
        each = max(2, -(-len(todo) // turns))
        events = [
            [functools.partial(arrival, *a) for a in todo[i * each : (i + 1) * each]]
            for i in range(turns)
        ]
        if k >= 1:
            events[3] += [functools.partial(outward, s) for s in groups[k - 1]]
        if k >= 2:
            events[5] += [functools.partial(own, s) for s in groups[k - 2]]
        product(groups[k][0], len(groups[k]), events)
        for s in groups[k]:
            exchange(s)
        if k == 1:
            to_other_core()
        if k == 2:
            transposed()
    outward(LAST)
    loads[5].wait()
    for s in groups[TOP - 1] + groups[TOP]:
        own(s)
    ur = take_recv(NX * NC * 2)
    most = NZ // NC - 1

    def rows_to(o, first, count, k):
        block = UF.at[d, pl.ds(first, count)]
        send(block, block, ur + d * 2 + k, at_xc(mod(x + o, NX), c))

    def up_grad_to_twin():
        for o in (1, 3, 2):
            e = mod(x + o, NX) * NC + c
            if o == 2:
                arrive(UF.at[e], ur + e * 2)
            else:
                arrive(UF.at[e, pl.ds(0, most)], ur + e * 2)
                arrive(UF.at[e, pl.ds(most, 1)], ur + e * 2 + 1)
            send(UF.at[e], UF.at[e], ur + e * 2, twin)

    def up_grad_from_twin():
        for o in range(NX):
            e = mod(x + o, NX) * NC + 1 - c
            arrive(UF.at[e], ur + e * 2)

    rows_to(1, 0, most, 0)
    rows_to(3, 0, most, 0)
    send(UF.at[d], UF.at[d], ur + d * 2, twin)

    r = TM.shape[1]
    part = r // NZ
    rows_own = XB.shape[1]

    def summed(src, first, second):
        r1, r2 = take_recv(NZ), take_recv(NY)
        first[z] = src[z]
        for o in (4, 3, 5, 2, 6, 1, 7):
            zz = mod(z + o, NZ)
            send(src.at[zz], first.at[z], r1 + z, at_yz(y, zz))
        for o in (1, 7, 2, 6, 3, 5, 4):
            zz = mod(z + o, NZ)
            arrive(first.at[zz], r1 + zz)
        v = first[0]
        for j in range(1, NZ):
            v = v + first[j]
        second[y] = v
        for o in (2, 1, 3):
            send(second.at[y], second.at[y], r2 + y, at_yz(mod(y + o, NY), z))
        for o in (1, 3, 2):
            yy = mod(y + o, NY)
            arrive(second.at[yy], r2 + yy)
        v = second[0]
        for j in range(1, NY):
            v = v + second[j]
        return v

    pairs = [(o, p) for o in (2, 1, 3, 0) for p in (4, 3, 5, 2, 6, 1, 7, 0) if o or p]

    def spread(full):
        base = take_recv(NX * NZ)
        for o, p in pairs:
            send(full.at[d, z], full.at[d, z], base + x * NZ + z, around(o, p))
        return base

    def collect(full, base):
        other = take_recv(NX)
        for o in (0, 1, 3, 2):
            xx = mod(x + o, NX)
            for p in (0, 1, 7, 2, 6, 3, 5, 4):
                if o or p:
                    zz = mod(z + p, NZ)
                    arrive(full.at[xx * NC + c, zz], base + xx * NZ + zz)
            send(full.at[xx * NC + c], full.at[xx * NC + c], other + xx, twin)
        return other

    def from_twin(full, other):
        for o in (0, 1, 3, 2):
            xx = mod(x + o, NX)
            arrive(full.at[xx * NC + 1 - c], other + xx)

    u = UF[d].reshape(rows_own, n)
    SP[...] = dot(u, TM[...], 1, 0).reshape(NZ, part, r)
    v = summed(SP, S1, S2)
    SF[d, z] = v
    base = spread(SF)
    rows_to(1, most, 1, 1)
    rows_to(3, most, 1, 1)
    rows_to(2, 0, most + 1, 0)
    other = collect(SF, base)
    from_twin(SF, other)

    s = SF[...].reshape(tokens, r)
    rc = jnp.zeros((XT.shape[0], r), F32)
    xt = XT[...]
    for piece in split3(s)[::-1]:
        rc = rc + dot(xt, piece, 1, 0)
    rc = rc * factor
    RC[...] = rc
    V[:, 0] = dot(rc, rc, 0, 0, HIGHEST).reshape(NZ, part, r)
    co = jnp.zeros((rows_own, r), F32)
    xown = XB[d]
    for piece in split3(rc)[::-1]:
        co = co + dot(xown, piece, 1, 0)
    V[:, 1] = co.reshape(NZ, part, r)
    v = summed(V, V1, V2)
    GF[z] = v[0]
    TF[d, z] = v[1]
    gr = take_recv(NZ)
    for o in (4, 3, 5, 2, 6, 1, 7):
        send(GF.at[z], GF.at[z], gr + z, at_yz(y, mod(z + o, NZ)))
    base = spread(TF)

    up_grad_to_twin()
    for o in (1, 7, 2, 6, 3, 5, 4):
        zz = mod(z + o, NZ)
        arrive(GF.at[zz], gr + zz)

    others = []
    inverse_factor(
        GF[...].reshape(r, r), WK, lambda: others.append(collect(TF, base))
    )
    inv = WK[:, r:]
    basis[...] = dot(RC[...], inv, 1, 1, HIGHEST) * math.sqrt(features)
    from_twin(TF, others[0])
    up_grad_from_twin()
    cot = dot(inv, TF[...].reshape(tokens, r), 1, 1, HIGHEST) * factor
    hi = cot.astype(BF16)
    low = (cot - hi.astype(F32)).astype(BF16)
    both = dot(jnp.concatenate([hi, low], axis=0), UF[...].reshape(tokens, n), 1, 0)
    corange[...] = both[:r] + both[r:]
    finish()


def shards(out_grad, down_weight, gate_pre, inputs, test_matrix):
    rows, depth = out_grad.shape
    n = down_weight.shape[0]
    own, width = inputs.shape
    r = test_matrix.shape[1]
    half = rows // 2
    part = r // NZ
    dp = NX * NC
    vm = pltpu.VMEM
    scratch = [
        vm((NZ * NY, rows, CUT), BF16),
        vm((NZ * NY, rows, depth - CUT), BF16),
        vm((n, depth), BF16),
        vm((own, n), BF16),
        vm((dp, own, width), BF16),
        vm((n, r), BF16),
        vm((NZ // NC, rows, n), F32),
        vm((NZ, 2, NY, half, n), F32),
        vm((NZ, NX - 1, half, n), F32),
        vm((NZ // NC, 2, half, n), F32),
        vm((NZ // NC, 2, half, n), F32),
        vm((NZ, NX - 1, half, n), BF16),
        vm((NX - 1, NZ // NC, 2, half, n), BF16),
        vm((dp, NZ // NC, 2, half, n), BF16),
        vm((width, dp * own), BF16),
        vm((NZ, part, r), F32),
        vm((NZ, part, r), F32),
        vm((NY, part, r), F32),
        vm((dp, NZ, part, r), F32),
        vm((width, r), F32),
        vm((NZ, 2, part, r), F32),
        vm((NZ, 2, part, r), F32),
        vm((NY, 2, part, r), F32),
        vm((NZ, part, r), F32),
        vm((dp, NZ, part, r), F32),
        vm((r, 2 * r), F32),
        pltpu.SemaphoreType.DMA((280,)),
        pltpu.SemaphoreType.DMA((280,)),
        pltpu.SemaphoreType.DMA((6,)),
    ]
    flops = 2 * dp * own * n * depth
    return pl.pallas_call(
        kernel,
        out_shape=(
            jax.ShapeDtypeStruct((width, r), F32),
            jax.ShapeDtypeStruct((r, n), F32),
        ),
        in_specs=[pl.BlockSpec(memory_space=pl.ANY)] * 5,
        out_specs=[pl.BlockSpec(memory_space=pltpu.VMEM)] * 2,
        scratch_shapes=scratch,
        cost_estimate=pl.CostEstimate(
            flops=flops, bytes_accessed=2 * n * depth, transcendentals=own * n
        ),
        compiler_params=pltpu.CompilerParams(
            collective_id=0, has_side_effects=True, vmem_limit_bytes=60 * 1024 * 1024
        ),
    )(out_grad, down_weight, gate_pre, inputs, test_matrix)


def solution(mesh):
    return jax.shard_map(
        shards,
        mesh=mesh,
        in_specs=(
            P("tensor", "dp"),
            P("tensor", "dp"),
            P("dp", "tensor"),
            P("dp", "tensor"),
            P("tensor", None),
        ),
        out_specs=(P("tensor", None), P(None, "tensor")),
        check_vma=False,
    )
```

time: 129 us -> 108 us (0.84)
  Pallas kernels: 124 us -> 103 us
    pallas_call x1, Pallas kernels: 124 us -> 103 us  [shards(): pl.pallas_call(kernel, out_shape=(jax.ShapeDtypeStruct((width, r), F32),...]
where the time goes in v2:
time: 108 us
  Pallas kernels  103 us (95%)
  local copies, waits for them, and re-layouts  3.78 us (4%)
    pallas_call x1, Pallas kernels, shards(): pl.pallas_call(kernel, out_shape=(jax.ShapeDtypeStruct((width, r), F32),...  103 us
    unnamed x2, local copies, waits for them, and re-layouts  3.78 us

profile of v2, /device:TPU:1, one launch (start us, length us, event | category | flops | bytes accessed | tf_op | source)
XLA Modules:
  0.0 107.6 jit_solution(9457346599247013921)
XLA Ops:
  0.6 103.2 %shard_map.68 = (f32[512,128]{1,0:T(8,128)}, f32[128,1664]{1,0:T(8,128)}) custom-call(bf16[32,2048]{1,0:T(8,128)(2,1)} %og.1, bf16[1664,2048]{1,0:T(8,128)(2,1)} %dw.1, bf16[128,1664]{1,0:T(8,128)(2,1)} %gate.1, bf16[128,512]{1,0:T(8,128)(2,1)} %inp.1, bf16[1664,128]{1,0:T(8,128)(2,1)} %test.1), custom_call_target="tpu_custom_call" | custom-call | flops 6979321856 | bytes 6815744 | tf_op jit(solution)/shard_map/pallas_call | solution.py:568
  103.8 1.7 %copy.9 = f32[512,128]{1,0:T(8,128)} copy(f32[512,128]{1,0:T(8,128)} %get-tuple-element.4) | data formatting | bytes 524288
  105.5 2.1 %copy.10 = f32[128,1664]{1,0:T(8,128)} copy(f32[128,1664]{1,0:T(8,128)} %get-tuple-element.5) | data formatting | bytes 1703936

commit v3 on v2

--- a/solution.py
+++ b/solution.py
@@ -63,7 +63,7 @@
 HIGHEST = lax.Precision.HIGHEST
 
 
-def inverse_factor(gram, work, midway):
+def inverse_factor(gram, work):
     n = gram.shape[0]
     ri = lax.broadcasted_iota(jnp.int32, (n, n), 0)
     ci = lax.broadcasted_iota(jnp.int32, (n, n), 1)
@@ -72,8 +72,6 @@
     sub = lax.broadcasted_iota(jnp.int32, (8, n), 0)
     sub2 = lax.broadcasted_iota(jnp.int32, (8, 2 * n), 0)
     for b in range(n // 8):
-        if b == n // 16:
-            midway()
         rows = slice(8 * b, 8 * b + 8)
         panel = work[rows, :]
         cols = [
@@ -101,8 +99,8 @@
 
 def kernel(
     og, dw, gate, inp, test, basis, corange,
-    GA, GB, W, GT, XB, TM, SIL, PT, SIBR, SIB0, HG, XS, RX, UF, XT,
-    SP, S1, S2, SF, RC, V, V1, V2, GF, TF, WK,
+    GA, GB, W, GT, XB, TM, SIL, PT, SIBR, SIB0, HG, XS, RX, UF,
+    SP, S1, S2, SF, RC, KP, KR, KY, TF, WK,
     sends, recvs, local,
 ):
     d, t = lax.axis_index("dp"), lax.axis_index("tensor")
@@ -133,7 +131,7 @@
     count = {"s": 0, "r": 0}
 
     def finish():
-        assert count["s"] <= 280 and count["r"] <= 280, count
+        assert count["s"] <= 340 and count["r"] <= 340, count
         for make, when in pending:
             if when is None:
                 make().wait_send()
@@ -347,6 +345,18 @@
             UF[d, zc] = (v * SIL[zc].reshape(2, half, n)).astype(BF16)
 
     groups = [[0]] + [[above(k), below(k)] for k in range(1, TOP)] + [[LAST]]
+    ur, tr = take_recv(NX * NC * (NZ // NC)), take_recv(NX * NC)
+    same_core = [at_xc(mod(x + o, NX), c) for o in range(NX)]
+    mine = [owners[s][0] == c for s in range(NZ)]
+    row_marks = [ur + d * (NZ // NC) + owners[s][1] for s in range(NZ)]
+
+    def rows_out(s):
+        core, zc = owners[s]
+        for o in (2, 1, 3):
+            send(
+                lambda: UF.at[d, zc], lambda: UF.at[d, zc], row_marks[s], same_core[o], mine[s]
+            )
+
     ends = [
         1 + max(i for i, a in enumerate(ARRIVALS) if a[0] in g) for g in groups
     ]
@@ -357,13 +367,44 @@
             arrive(XB.at[e], xr + e)
             send(XB.at[e], XB.at[e], xr + e, twin)
 
-    def transposed():
-        rows = XB.shape[1]
+    def inner_terms():
+        rows, width = XB.shape[1], XB.shape[2]
         for o in range(NX):
             e = mod(x + o, NX) * NC + 1 - c
             arrive(XB.at[e], xr + e)
-        for e in range(NX * NC):
-            XT[:, e * rows : (e + 1) * rows] = XB[e].T
+        v = dot(XB[d], XB[...].reshape(NX * NC * rows, width), 1, 1)
+        part, wide = KP.shape[2], KP.shape[3]
+        for zz in range(NZ):
+            for yy in range(NY):
+                KP[zz, yy] = v[
+                    zz * part : (zz + 1) * part, yy * wide : (yy + 1) * wide
+                ]
+
+    kr, ky = take_recv(NY * NZ), take_recv(NY)
+    hops = [(o, p) for p in (4, 3, 5, 2, 6, 1, 7, 0) for o in (2, 1, 3, 0) if o or p]
+
+    def inner_out():
+        for o, p in hops:
+            yy, zz = mod(y + o, NY), mod(z + p, NZ)
+            send(KP.at[zz, yy], KR.at[t], kr + t, at_yz(yy, zz))
+        KR[t] = KP[z, y]
+
+    def inner_sum():
+        for o, p in hops[::-1]:
+            tt = mod(y + o, NY) * NZ + mod(z + p, NZ)
+            arrive(KR.at[tt], kr + tt)
+        v = KR[0]
+        for j in range(1, NY * NZ):
+            v = v + KR[j]
+        KY[y] = v
+        for o in (2, 1, 3):
+            send(KY.at[y], KY.at[y], ky + y, at_yz(mod(y + o, NY), z))
+
+    def inner_rows():
+        for o in (1, 3, 2):
+            yy = mod(y + o, NY)
+            arrive(KY.at[yy], ky + yy)
+        return jnp.concatenate([KY[j] for j in range(NY)], axis=1)
 
     loads[3].wait()
     g = GT[...].astype(F32)
@@ -382,49 +423,45 @@
         if k >= 1:
             events[3] += [functools.partial(outward, s) for s in groups[k - 1]]
         if k >= 2:
-            events[5] += [functools.partial(own, s) for s in groups[k - 2]]
+            for s in groups[k - 2]:
+                events[5].append(functools.partial(own, s))
+                if k < TOP:
+                    events[5].append(functools.partial(rows_out, s))
+        if k == TOP:
+            inner_out()
         product(groups[k][0], len(groups[k]), events)
         for s in groups[k]:
             exchange(s)
         if k == 1:
             to_other_core()
         if k == 2:
-            transposed()
+            inner_terms()
     outward(LAST)
     loads[5].wait()
     for s in groups[TOP - 1] + groups[TOP]:
         own(s)
-    ur = take_recv(NX * NC * 2)
-    most = NZ // NC - 1
-
-    def rows_to(o, first, count, k):
-        block = UF.at[d, pl.ds(first, count)]
-        send(block, block, ur + d * 2 + k, at_xc(mod(x + o, NX), c))
+    for k in range(TOP - 2, TOP + 1):
+        for s in groups[k]:
+            rows_out(s)
+    send(UF.at[d], UF.at[d], tr + d, twin)
 
     def up_grad_to_twin():
         for o in (1, 3, 2):
             e = mod(x + o, NX) * NC + c
-            if o == 2:
-                arrive(UF.at[e], ur + e * 2)
-            else:
-                arrive(UF.at[e, pl.ds(0, most)], ur + e * 2)
-                arrive(UF.at[e, pl.ds(most, 1)], ur + e * 2 + 1)
-            send(UF.at[e], UF.at[e], ur + e * 2, twin)
+            for zc in range(NZ // NC):
+                arrive(UF.at[e, zc], ur + e * (NZ // NC) + zc)
+            send(UF.at[e], UF.at[e], tr + e, twin)
 
     def up_grad_from_twin():
         for o in range(NX):
             e = mod(x + o, NX) * NC + 1 - c
-            arrive(UF.at[e], ur + e * 2)
-
-    rows_to(1, 0, most, 0)
-    rows_to(3, 0, most, 0)
-    send(UF.at[d], UF.at[d], ur + d * 2, twin)
+            arrive(UF.at[e], tr + e)
 
     r = TM.shape[1]
     part = r // NZ
     rows_own = XB.shape[1]
 
-    def summed(src, first, second):
+    def summed(src, first, second, between):
         r1, r2 = take_recv(NZ), take_recv(NY)
         first[z] = src[z]
         for o in (4, 3, 5, 2, 6, 1, 7):
@@ -439,6 +476,7 @@
         second[y] = v
         for o in (2, 1, 3):
             send(second.at[y], second.at[y], r2 + y, at_yz(mod(y + o, NY), z))
+        between()
         for o in (1, 3, 2):
             yy = mod(y + o, NY)
             arrive(second.at[yy], r2 + yy)
@@ -473,55 +511,51 @@
 
     u = UF[d].reshape(rows_own, n)
     SP[...] = dot(u, TM[...], 1, 0).reshape(NZ, part, r)
-    v = summed(SP, S1, S2)
+    v = summed(SP, S1, S2, inner_sum)
     SF[d, z] = v
     base = spread(SF)
-    rows_to(1, most, 1, 1)
-    rows_to(3, most, 1, 1)
-    rows_to(2, 0, most + 1, 0)
+    inner = inner_rows()
     other = collect(SF, base)
     from_twin(SF, other)
 
     s = SF[...].reshape(tokens, r)
-    rc = jnp.zeros((XT.shape[0], r), F32)
-    xt = XT[...]
-    for piece in split3(s)[::-1]:
-        rc = rc + dot(xt, piece, 1, 0)
-    rc = rc * factor
-    RC[...] = rc
-    V[:, 0] = dot(rc, rc, 0, 0, HIGHEST).reshape(NZ, part, r)
-    co = jnp.zeros((rows_own, r), F32)
-    xown = XB[d]
-    for piece in split3(rc)[::-1]:
-        co = co + dot(xown, piece, 1, 0)
-    V[:, 1] = co.reshape(NZ, part, r)
-    v = summed(V, V1, V2)
-    GF[z] = v[0]
-    TF[d, z] = v[1]
-    gr = take_recv(NZ)
-    for o in (4, 3, 5, 2, 6, 1, 7):
-        send(GF.at[z], GF.at[z], gr + z, at_yz(y, mod(z + o, NZ)))
+    TF[d, z] = dot(inner, s, 1, 0, HIGHEST) * factor
     base = spread(TF)
 
+    every = XB[...].reshape(tokens, XB.shape[2])
+    rc = dot(every, jnp.concatenate(split3(s), axis=1), 0, 0)
+    RC[...] = (rc[:, :r] + (rc[:, r : 2 * r] + rc[:, 2 * r :])) * factor
     up_grad_to_twin()
-    for o in (1, 7, 2, 6, 3, 5, 4):
-        zz = mod(z + o, NZ)
-        arrive(GF.at[zz], gr + zz)
-
-    others = []
-    inverse_factor(
-        GF[...].reshape(r, r), WK, lambda: others.append(collect(TF, base))
-    )
+    from_twin(TF, collect(TF, base))
+    tt = TF[...].reshape(tokens, r)
+    inverse_factor(dot(SF[...].reshape(tokens, r), tt, 0, 0, HIGHEST) * factor, WK)
     inv = WK[:, r:]
     basis[...] = dot(RC[...], inv, 1, 1, HIGHEST) * math.sqrt(features)
-    from_twin(TF, others[0])
     up_grad_from_twin()
-    cot = dot(inv, TF[...].reshape(tokens, r), 1, 1, HIGHEST) * factor
+    cot = dot(inv, tt, 1, 1, HIGHEST) * factor
     hi = cot.astype(BF16)
     low = (cot - hi.astype(F32)).astype(BF16)
     both = dot(jnp.concatenate([hi, low], axis=0), UF[...].reshape(tokens, n), 1, 0)
     corange[...] = both[:r] + both[r:]
     finish()
+
+
+def hand_over(basis_in, corange_in, basis, corange, basis_held, corange_held, done):
+    into = [
+        pltpu.make_async_copy(basis_in, basis_held, done.at[0]),
+        pltpu.make_async_copy(corange_in, corange_held, done.at[1]),
+    ]
+    out = [
+        pltpu.make_async_copy(basis_held, basis, done.at[2]),
+        pltpu.make_async_copy(corange_held, corange, done.at[3]),
+    ]
+    for cp in into:
+        cp.start()
+    for first, second in zip(into, out):
+        first.wait()
+        second.start()
+    for cp in out:
+        cp.wait()
 
 
 def shards(out_grad, down_weight, gate_pre, inputs, test_matrix):
@@ -548,24 +582,22 @@
         vm((NZ, NX - 1, half, n), BF16),
         vm((NX - 1, NZ // NC, 2, half, n), BF16),
         vm((dp, NZ // NC, 2, half, n), BF16),
-        vm((width, dp * own), BF16),
         vm((NZ, part, r), F32),
         vm((NZ, part, r), F32),
         vm((NY, part, r), F32),
         vm((dp, NZ, part, r), F32),
         vm((width, r), F32),
-        vm((NZ, 2, part, r), F32),
-        vm((NZ, 2, part, r), F32),
-        vm((NY, 2, part, r), F32),
-        vm((NZ, part, r), F32),
+        vm((NZ, NY, part, dp * own // NY), F32),
+        vm((NY * NZ, part, dp * own // NY), F32),
+        vm((NY, part, dp * own // NY), F32),
         vm((dp, NZ, part, r), F32),
         vm((r, 2 * r), F32),
-        pltpu.SemaphoreType.DMA((280,)),
-        pltpu.SemaphoreType.DMA((280,)),
+        pltpu.SemaphoreType.DMA((340,)),
+        pltpu.SemaphoreType.DMA((340,)),
         pltpu.SemaphoreType.DMA((6,)),
     ]
     flops = 2 * dp * own * n * depth
-    return pl.pallas_call(
+    results = pl.pallas_call(
         kernel,
         out_shape=(
             jax.ShapeDtypeStruct((width, r), F32),
@@ -581,6 +613,15 @@
             collective_id=0, has_side_effects=True, vmem_limit_bytes=60 * 1024 * 1024
         ),
     )(out_grad, down_weight, gate_pre, inputs, test_matrix)
+    anywhere = pl.BlockSpec(memory_space=pl.ANY)
+    return pl.pallas_call(
+        hand_over,
+        out_shape=tuple(jax.ShapeDtypeStruct(a.shape, a.dtype) for a in results),
+        in_specs=[anywhere] * 2,
+        out_specs=[anywhere] * 2,
+        scratch_shapes=[pltpu.VMEM(a.shape, a.dtype) for a in results]
+        + [pltpu.SemaphoreType.DMA((4,))],
+    )(*results)
 
 
 def solution(mesh):

time: 108 us -> 106 us (0.981)
  local copies, waits for them, and re-layouts: 3.78 us -> 0 us
  Pallas kernels: 103 us -> 105 us
    unnamed x2 -> x0, local copies, waits for them, and re-layouts: 3.78 us -> none
    pallas_call x0 -> x1, Pallas kernels: none -> 2.18 us  [shards(): pl.pallas_call(hand_over, out_shape=tuple((jax.ShapeDtypeStruct(a.shape,...]
where the time goes in v3:
time: 106 us
  Pallas kernels  105 us (99%)
    pallas_call x1, Pallas kernels, shards(): pl.pallas_call(kernel, out_shape=(jax.ShapeDtypeStruct((width, r), F32),...  103 us
    pallas_call x1, Pallas kernels, shards(): pl.pallas_call(hand_over, out_shape=tuple((jax.ShapeDtypeStruct(a.shape,...  2.18 us

profile of v3, /device:TPU:1, one launch (start us, length us, event | category | flops | bytes accessed | tf_op | source)
XLA Modules:
  0.0 105.6 jit_solution(13368985375244939940)
XLA Ops:
  0.6 102.6 %shard_map.68 = (f32[512,128]{1,0:T(8,128)}, f32[128,1664]{1,0:T(8,128)}) custom-call(bf16[32,2048]{1,0:T(8,128)(2,1)} %og.1, bf16[1664,2048]{1,0:T(8,128)(2,1)} %dw.1, bf16[128,1664]{1,0:T(8,128)(2,1)} %gate.1, bf16[128,512]{1,0:T(8,128)(2,1)} %inp.1, bf16[1664,128]{1,0:T(8,128)(2,1)} %test.1), custom_call_target="tpu_custom_call" | custom-call | flops 6979321856 | bytes 6815744 | tf_op jit(solution)/shard_map/pallas_call | solution.py:600
  103.3 2.2 %shard_map.69 = (f32[512,128]{1,0:T(8,128)}, f32[128,1664]{1,0:T(8,128)}) custom-call(f32[512,128]{1,0:T(8,128)} %get-tuple-element.4.basis_in, f32[128,1664]{1,0:T(8,128)} %get-tuple-element.5.corange_in), custom_call_target="tpu_custom_call" | custom-call | tf_op jit(solution)/shard_map/pallas_call | solution.py:617

commit v4 on v3

--- a/solution.py
+++ b/solution.py
@@ -422,23 +422,21 @@
         ]
         if k >= 1:
             events[3] += [functools.partial(outward, s) for s in groups[k - 1]]
-        if k >= 2:
-            for s in groups[k - 2]:
-                events[5].append(functools.partial(own, s))
-                if k < TOP:
-                    events[5].append(functools.partial(rows_out, s))
+        if k == TOP:
+            for s in groups[0] + groups[1]:
+                events[5] += [functools.partial(own, s), functools.partial(rows_out, s)]
         if k == TOP:
             inner_out()
         product(groups[k][0], len(groups[k]), events)
         for s in groups[k]:
             exchange(s)
-        if k == 1:
+        if k == 2:
             to_other_core()
-        if k == 2:
+        if k == 3:
             inner_terms()
     outward(LAST)
     loads[5].wait()
-    for s in groups[TOP - 1] + groups[TOP]:
+    for s in groups[TOP - 2] + groups[TOP - 1] + groups[TOP]:
         own(s)
     for k in range(TOP - 2, TOP + 1):
         for s in groups[k]:

time: 106 us -> 106 us (level)
  no operation moved by 1% of the time
where the time goes in v4:
time: 106 us
  Pallas kernels  105 us (99%)
    pallas_call x1, Pallas kernels, shards(): pl.pallas_call(kernel, out_shape=(jax.ShapeDtypeStruct((width, r), F32),...  103 us
    pallas_call x1, Pallas kernels, shards(): pl.pallas_call(hand_over, out_shape=tuple((jax.ShapeDtypeStruct(a.shape,...  2.18 us

profile of v4, /device:TPU:1, one launch (start us, length us, event | category | flops | bytes accessed | tf_op | source)
XLA Modules:
  0.0 105.6 jit_solution(15561318179493741775)
XLA Ops:
  0.6 102.6 %shard_map.68 = (f32[512,128]{1,0:T(8,128)}, f32[128,1664]{1,0:T(8,128)}) custom-call(bf16[32,2048]{1,0:T(8,128)(2,1)} %og.1, bf16[1664,2048]{1,0:T(8,128)(2,1)} %dw.1, bf16[128,1664]{1,0:T(8,128)(2,1)} %gate.1, bf16[128,512]{1,0:T(8,128)(2,1)} %inp.1, bf16[1664,128]{1,0:T(8,128)(2,1)} %test.1), custom_call_target="tpu_custom_call" | custom-call | flops 6979321856 | bytes 6815744 | tf_op jit(solution)/shard_map/pallas_call | solution.py:598
  103.3 2.2 %shard_map.69 = (f32[512,128]{1,0:T(8,128)}, f32[128,1664]{1,0:T(8,128)}) custom-call(f32[512,128]{1,0:T(8,128)} %get-tuple-element.4.basis_in, f32[128,1664]{1,0:T(8,128)} %get-tuple-element.5.corange_in), custom_call_target="tpu_custom_call" | custom-call | tf_op jit(solution)/shard_map/pallas_call | solution.py:615
